TPU v7x, 256 devices: a whole 4x4x8 slice. The times are simulated.
256 devices in a mesh: ea: 128 (over y, z, x), ta: 2 (over core).
Axes of the slice: x: 4, y: 4, z: 8, core: 2. Of those that a mesh axis runs over, the one named last changes fastest.
Arguments:
- sample_inphase: float32 [128, 256, 256], P('ea'), may hold values from 0.2 to 1.2
- sample_quadrature: float32 [128, 256, 256], P('ea'), may hold values from -3 to 3
- beam_inphase: float32 [128, 3, 32, 32], P('ea'), may hold values from -3 to 3
- beam_quadrature: float32 [128, 3, 32, 32], P('ea'), may hold values from -3 to 3
- recorded_diffraction: float32 [128, 2, 16, 32, 32], P('ea', 'ta'), may hold values from 0.05 to 4
- window_corners: int32 [128, 2, 16, 2], P('ea', 'ta'), may hold values from 0 to 224
- filled_tallies: int32 [128, 2], P('ea', 'ta'), may hold values from 1 to 16, 24 in all within a row
- absorption_templates: float32 [16, 128], replicated, may hold values from -6 to 6
Outputs:
- fitted: float32 [2, 128, 128, 2, 256], P(None, 'ea', None, 'ta')
- coefficients: float32 [2, 16, 65536], P(None, None, ('ea', 'ta'))
Inputs may be any that keep to these rules, and one draw needn't show every extreme that they name: `filled_tallies`: in each energy the two tiles' counts sum to 24 and the larger is at most 16. `window_corners`: offsets of slots at or past their tile's count are not used.
All inputs are finite; a program needn't handle non-finite values. No bound on the sum of `filled_tallies` on one device may be relied on, other than what follows from the above.
Results may differ from a plain program's by a relative error of at most 0.0003.
Values sent between devices are 32-bit elements; how exact they have to be, the bound alone decides.
A program may use at most 64 MiB of HBM per device.

v0:
```python
import jax
import jax.numpy as jnp
from jax import lax
from jax.sharding import PartitionSpec as P

HIGHEST_PRECISION = lax.Precision.HIGHEST
FLOOR_POWER = 0.5
REGULARIZER = 1.0


def dft_tables(length):
    counter = jnp.arange(length, dtype=jnp.int32)
    product = counter[:, None] * counter[None, :] % length
    angles = 2.0 * jnp.pi / length * product.astype(jnp.float32)
    norming = 1.0 / jnp.sqrt(jnp.float32(length))
    return (jnp.cos(angles) * norming, -jnp.sin(angles) * norming)


def two_sided(field_re, field_im, table_re, table_im):
    left_re = jnp.einsum(
        "jk,...kl->...jl", table_re, field_re, precision=HIGHEST_PRECISION
    ) - jnp.einsum("jk,...kl->...jl", table_im, field_im, precision=HIGHEST_PRECISION)
    left_im = jnp.einsum(
        "jk,...kl->...jl", table_re, field_im, precision=HIGHEST_PRECISION
    ) + jnp.einsum("jk,...kl->...jl", table_im, field_re, precision=HIGHEST_PRECISION)
    right_re = jnp.einsum(
        "...jk,kl->...jl", left_re, table_re, precision=HIGHEST_PRECISION
    ) - jnp.einsum("...jk,kl->...jl", left_im, table_im, precision=HIGHEST_PRECISION)
    right_im = jnp.einsum(
        "...jk,kl->...jl", left_re, table_im, precision=HIGHEST_PRECISION
    ) + jnp.einsum("...jk,kl->...jl", left_im, table_re, precision=HIGHEST_PRECISION)
    return (right_re, right_im)


def slot_terms(
    sample_inphase,
    sample_quadrature,
    beam_inphase,
    beam_quadrature,
    intensity,
    corners,
    weight,
    table_re,
    table_im,
):
    width = beam_inphase.shape[-1]

    def extract(source, corner):
        return lax.dynamic_slice(source, (corner[0], corner[1]), (width, width))

    patch_re = jax.vmap(extract, (None, 0))(sample_inphase, corners)
    patch_im = jax.vmap(extract, (None, 0))(sample_quadrature, corners)
    exit_re = beam_inphase[None] * patch_re[:, None] - beam_quadrature[None] * patch_im[:, None]
    exit_im = beam_inphase[None] * patch_im[:, None] + beam_quadrature[None] * patch_re[:, None]
    far_re, far_im = two_sided(exit_re, exit_im, table_re, table_im)
    power = jnp.sum(far_re * far_re + far_im * far_im, axis=1)
    factor = (1.0 - jnp.sqrt(intensity) / jnp.sqrt(jnp.maximum(power, FLOOR_POWER))) * weight[
        :, None, None
    ]
    back_re, back_im = two_sided(
        far_re * factor[:, None], far_im * factor[:, None], table_re, -table_im
    )
    terms_re = jnp.sum(beam_inphase[None] * back_re + beam_quadrature[None] * back_im, axis=1)
    terms_im = jnp.sum(beam_inphase[None] * back_im - beam_quadrature[None] * back_re, axis=1)
    return (terms_re, terms_im)


def deposit(field, patch, corner):
    width = patch.shape[0]
    current = lax.dynamic_slice(field, (corner[0], corner[1]), (width, width))
    return lax.dynamic_update_slice(field, current + patch, (corner[0], corner[1]))


def local(
    sample_inphase,
    sample_quadrature,
    beam_inphase,
    beam_quadrature,
    recorded_diffraction,
    window_corners,
    filled_tallies,
    absorption_templates,
):
    local_energies = sample_inphase.shape[0]
    side = sample_inphase.shape[1]
    spot_numbering = recorded_diffraction.shape[2]
    width = beam_inphase.shape[-1]
    blocks = lax.axis_size("ea")
    tiles = lax.axis_size("ta")
    tile = lax.axis_index("ta")
    table_re, table_im = dft_tables(width)
    group = 8
    first_slot = jnp.zeros((local_energies,), jnp.int32)
    taken_slots = filled_tallies[:, 0]
    tile_boundary = jnp.full((local_energies,), spot_numbering, jnp.int32)
    gathered_recordings = recorded_diffraction[:, 0]
    pooled_offsets = window_corners[:, 0]

    def lone_wavelength(items):
        o_re, o_im, p_re, p_im, intensity_pool, corner_pool, start, number, split = items
        light_patch = jnp.sum(p_re * p_re + p_im * p_im, axis=0)
        zeros = jnp.zeros((side, side), jnp.float32)

        def advance(index, carry):
            grad_re, grad_im, light = carry
            position = start + index * group + jnp.arange(group, dtype=jnp.int32)
            weight = (position < start + number).astype(jnp.float32)
            source = jnp.where(position < split, position, spot_numbering + position - split)
            source = jnp.clip(source, 0, intensity_pool.shape[0] - 1)
            corners = corner_pool[source]
            terms_re, terms_im = slot_terms(
                o_re, o_im, p_re, p_im, intensity_pool[source], corners, weight, table_re, table_im
            )
            for member in range(group):
                grad_re = deposit(grad_re, terms_re[member], corners[member])
                grad_im = deposit(grad_im, terms_im[member], corners[member])
                light = deposit(light, light_patch * weight[member], corners[member])
            return (grad_re, grad_im, light)

        rounds = (number + group - 1) // group
        return lax.fori_loop(0, rounds, advance, (zeros, zeros, zeros))

    grad_re, grad_im, light = lax.map(
        lone_wavelength,
        (
            sample_inphase,
            sample_quadrature,
            beam_inphase,
            beam_quadrature,
            gathered_recordings,
            pooled_offsets,
            first_slot,
            taken_slots,
            tile_boundary,
        ),
    )

    def shares(field):
        return field.reshape(local_energies, blocks, tiles, -1)

    summed = lax.psum_scatter(
        jnp.stack([shares(grad_re), shares(grad_im), shares(light)]),
        "ta",
        scatter_dimension=3,
        tiled=True,
    )
    light_share = summed[2]
    own_re = lax.dynamic_slice_in_dim(shares(sample_inphase), tile, 1, 2)
    own_im = lax.dynamic_slice_in_dim(shares(sample_quadrature), tile, 1, 2)
    revised_inphase = own_re - summed[0] / (light_share + REGULARIZER)
    revised_quadrature = own_im - summed[1] / (light_share + REGULARIZER)
    spectra = jnp.stack([revised_inphase, revised_quadrature])[:, :, :, 0, :]
    gram = jnp.dot(absorption_templates, absorption_templates.T, precision=HIGHEST_PRECISION)
    factor_low = jnp.linalg.cholesky(gram)
    project = jax.scipy.linalg.cho_solve((factor_low, True), absorption_templates)
    values = lax.all_to_all(spectra, "ea", split_axis=2, concat_axis=1, tiled=True)[:, :, 0, :]
    coefs = jnp.einsum("ke,cen->ckn", project, values, precision=HIGHEST_PRECISION)
    fitted_here = jnp.einsum(
        "ke,ckn->cen", absorption_templates, coefs, precision=HIGHEST_PRECISION
    )
    returned = lax.all_to_all(
        fitted_here[:, :, None, :], "ea", split_axis=1, concat_axis=2, tiled=True
    )
    coef_local = coefs[:, :, None, :]
    return (returned[:, :, :, None, :], coef_local[:, :, 0, :])


def solution(mesh):
    in_specs = (
        P("ea", None, None),
        P("ea", None, None),
        P("ea", None, None, None),
        P("ea", None, None, None),
        P("ea", "ta", None, None, None),
        P("ea", "ta", None, None),
        P("ea", "ta"),
        P(),
    )
    out_specs = (P(None, "ea", None, "ta", None), P(None, None, ("ea", "ta")))
    return jax.shard_map(local, mesh=mesh, in_specs=in_specs, out_specs=out_specs, check_vma=False)
```

profile of v0, /device:TPU:2, one launch (start us, length us, event | category | flops | bytes accessed | tf_op | source)
XLA Modules:
  0.0 321.7 jit_solution(4731289166006635438)
XLA Ops:
  10.6 216.4 %while.42 = (s32[]{:T(128)}, f32[256,256]{1,0:T(8,128)S(1)}, f32[256,256]{1,0:T(8,128)S(1)}, f32[256,256]{1,0:T(8,128)S(1)}, s32[]{:T(128)}, /*index=5*/s32[16,2...) while((s32[]{:T(128)}, f32[256,256]{1,0:T(8,128)S(1)}, ...), condition=%wide.region_5.6_spmd.clone.clone, body=%wide.region_1.5_spmd.clone.clone.sunk | while | flops 152179840 | bytes 5044471 | solution.py:121
  18.2 1.1 dynamic_update_slice.335
  29.1 1.1 dynamic_update_slice.337
  34.5 1.1 dynamic_update_slice.338
  57.4 14.9 %while.44 = (s32[]{:T(128)}, f32[256,256]{1,0:T(8,128)S(1)}, s32[8,2]{0,1:T(2,128)S(1)}, f32[8,32,32]{2,1,0:T(8,128)S(1)}, s32[]{:T(128)}) while((s32[]{:T(128)}, f32[256,256]{1,0:T(8,128)S(1)}, s32[8,2]{0,1:T(2,128)S(1)}, f32[8,32,32]{2,1,0:T(8,128)S(1)}, s32[]{:T(128)}) %tuple.143), condition=%wide.while_cond, body=%wide.while_body.sunk | while | flops 2 | bytes 32877 | solution.py:49
  58.0 1.3 bitcast_dynamic-update-slice_fusion.5
  59.9 1.3 bitcast_dynamic-update-slice_fusion.5
  61.7 1.3 bitcast_dynamic-update-slice_fusion.5
  63.6 1.3 bitcast_dynamic-update-slice_fusion.5
  65.5 1.3 bitcast_dynamic-update-slice_fusion.5
  67.3 1.3 bitcast_dynamic-update-slice_fusion.5
  69.2 1.3 bitcast_dynamic-update-slice_fusion.5
  71.0 1.3 bitcast_dynamic-update-slice_fusion.5
  72.3 14.9 %while.43 = (s32[]{:T(128)}, f32[256,256]{1,0:T(8,128)S(1)}, s32[8,2]{0,1:T(2,128)S(1)}, f32[8,32,32]{2,1,0:T(8,128)S(1)}, s32[]{:T(128)}) while((s32[]{:T(128)}, f32[256,256]{1,0:T(8,128)S(1)}, s32[8,2]{0,1:T(2,128)S(1)}, f32[8,32,32]{2,1,0:T(8,128)S(1)}, s32[]{:T(128)}) %tuple.153), condition=%wide.while_cond.1, body=%wide.while_body.1.sunk | while | flops 2 | bytes 32877 | solution.py:49
  72.9 1.3 bitcast_dynamic-update-slice_fusion.4
  74.8 1.3 bitcast_dynamic-update-slice_fusion.4
  76.7 1.3 bitcast_dynamic-update-slice_fusion.4
  78.5 1.3 bitcast_dynamic-update-slice_fusion.4
  80.4 1.3 bitcast_dynamic-update-slice_fusion.4
  82.2 1.3 bitcast_dynamic-update-slice_fusion.4
  84.1 1.3 bitcast_dynamic-update-slice_fusion.4
  86.0 1.3 bitcast_dynamic-update-slice_fusion.4
  100.9 1.1 dynamic_update_slice.327
  107.6 1.1 dynamic_update_slice.333
  109.6 1.1 dynamic_update_slice.319
  112.0 1.1 dynamic_update_slice.321
  113.2 1.1 dynamic_update_slice.322
  116.3 1.1 dynamic_update_slice.325
  131.3 1.1 dynamic_update_slice.336
  142.3 1.1 dynamic_update_slice.338
  147.8 1.1 dynamic_update_slice.339
  164.1 1.1 dynamic_update_slice.342
  165.4 14.9 %while.44 = (s32[]{:T(128)}, f32[256,256]{1,0:T(8,128)S(1)}, s32[8,2]{0,1:T(2,128)S(1)}, f32[8,32,32]{2,1,0:T(8,128)S(1)}, s32[]{:T(128)}) while((s32[]{:T(128)}, f32[256,256]{1,0:T(8,128)S(1)}, s32[8,2]{0,1:T(2,128)S(1)}, f32[8,32,32]{2,1,0:T(8,128)S(1)}, s32[]{:T(128)}) %tuple.143), condition=%wide.while_cond, body=%wide.while_body.sunk | while | flops 2 | bytes 32877 | solution.py:49
  166.0 1.3 bitcast_dynamic-update-slice_fusion.5
  167.9 1.3 bitcast_dynamic-update-slice_fusion.5
  169.7 1.3 bitcast_dynamic-update-slice_fusion.5
  171.6 1.3 bitcast_dynamic-update-slice_fusion.5
  173.5 1.3 bitcast_dynamic-update-slice_fusion.5
  175.3 1.3 bitcast_dynamic-update-slice_fusion.5
  177.2 1.3 bitcast_dynamic-update-slice_fusion.5
  179.0 1.3 bitcast_dynamic-update-slice_fusion.5
  180.3 14.9 %while.43 = (s32[]{:T(128)}, f32[256,256]{1,0:T(8,128)S(1)}, s32[8,2]{0,1:T(2,128)S(1)}, f32[8,32,32]{2,1,0:T(8,128)S(1)}, s32[]{:T(128)}) while((s32[]{:T(128)}, f32[256,256]{1,0:T(8,128)S(1)}, s32[8,2]{0,1:T(2,128)S(1)}, f32[8,32,32]{2,1,0:T(8,128)S(1)}, s32[]{:T(128)}) %tuple.153), condition=%wide.while_cond.1, body=%wide.while_body.1.sunk | while | flops 2 | bytes 32877 | solution.py:49
  180.9 1.3 bitcast_dynamic-update-slice_fusion.4
  182.8 1.3 bitcast_dynamic-update-slice_fusion.4
  184.7 1.3 bitcast_dynamic-update-slice_fusion.4
  186.5 1.3 bitcast_dynamic-update-slice_fusion.4
  188.4 1.3 bitcast_dynamic-update-slice_fusion.4
  190.2 1.3 bitcast_dynamic-update-slice_fusion.4
  192.1 1.3 bitcast_dynamic-update-slice_fusion.4
  194.0 1.3 bitcast_dynamic-update-slice_fusion.4
  208.9 1.1 dynamic_update_slice.327
  210.1 1.1 dynamic_update_slice.328
  211.3 1.1 dynamic_update_slice.329
  212.5 1.1 dynamic_update_slice.330
  213.7 1.1 dynamic_update_slice.331
  217.9 1.1 dynamic_update_slice.319
  219.1 1.1 dynamic_update_slice.320
  229.6 1.5 cholesky.16
  233.0 28.8 %all-reduce.3.cloned.1.call-done = f32[3,1,128,2,256]{4,2,3,1,0:T(8,128)} async-done(((f32[3,1,128,2,256]{4,2,3,1,0:T(8,128)}), f32[3,1,128,2,256]{4,2,3,1,0:T(8,128)}) %all-reduce.3.cloned.1.call-update) | async-done | bytes 786448
  261.8 1.7 constant_dynamic-slice_fusion.3
  264.9 13.8 %all-to-all-start = ((f32[2,1,128,256]{3,0,1,2:T(2,128)}), f32[2,1,128,256]{3,0,1,2:T(2,128)S(1)}, u32[]{:S(2)}, u32[]{:S(2)}) async-start(f32[2,1,128,256]{3,0,1,2:T(2,128)} %maximum_bitcast_fusion), calls=%async_computation | async-start | bytes 524288 | tf_op jit(solution)/shard_map/all_to_all | solution.py:156
  279.3 1.2 custom-call.10
  280.9 12.0 %all-to-all-done = f32[2,1,128,256]{3,0,1,2:T(2,128)S(1)} async-done(((f32[2,1,128,256]{3,0,1,2:T(2,128)}), f32[2,1,128,256]{3,0,1,2:T(2,128)S(1)}, u32[]{:S(2)}, u32[]{:S(2)}) %all-to-all-start) | async-done | bytes 262176 | tf_op jit(solution)/shard_map/all_to_all | solution.py:156
  294.0 19.9 %all_to_all.8 = f32[2,128,1,256]{3,0,2,1:T(2,128)S(1)} all-to-all(f32[2,128,1,256]{3,0,2,1:T(2,128)S(1)} %copy.85), channel_id=1, replica_groups=mesh['ea'=128,'ta'=2] {'ea'}, dimensions={1} | all-to-all | bytes 524288 | tf_op jit(solution)/shard_map/all_to_all | solution.py:161
  (245 shorter events, 104.9 us)
Async XLA Ops:
  7.2 222.2 %copy-start = (f32[16,128]{1,0:T(8,128)S(1)}, f32[16,128]{1,0:T(8,128)}, u32[]{:S(2)}) copy-start(f32[16,128]{1,0:T(8,128)} %param.17) | copy-start | bytes 24580
  7.2 254.6 %all-reduce.3.cloned.1.call-start = ((), (), s32[]{:S(2)}) async-start(), calls=%async_computation.2 | async-start | bytes 1572864
  7.9 0.7 copy-start.7
  8.7 1.0 copy-start.5
  9.5 1.0 copy-start.4
  9.6 1.0 copy-start.3
  9.6 1.0 copy-start.1
  9.6 1.0 copy-start.2
  231.1 0.7 copy-start.8
  264.9 28.0 %all-to-all-start = ((f32[2,1,128,256]{3,0,1,2:T(2,128)}), f32[2,1,128,256]{3,0,1,2:T(2,128)S(1)}, u32[]{:S(2)}, u32[]{:S(2)}) async-start(f32[2,1,128,256]{3,0,1,2:T(2,128)} %maximum_bitcast_fusion), calls=%async_computation | async-start | bytes 524288 | tf_op jit(solution)/shard_map/all_to_all | solution.py:156
  293.2 0.6 copy-start.6
Sparse Core Ops, SparseCore 0:
  229.0 32.7 all-reduce.2
where the time goes:
time: 325 us; the launch traced here: 322 us
  local copies, waits for them, and re-layouts  122 us (38%)
  loops' own time  60.9 us (19%)
  waiting for transfers between devices  40.8 us (13%)
  matrix products  27 us (8%)
  other arithmetic  22.7 us (7%)
  blocking collectives  19.9 us (6%)
  between operations  14.9 us (5%)
  starting transfers between devices  13.8 us (4%)
    another operation x1, loops' own time, lone_wavelength(): return lax.fori_loop(0, rounds, advance, (zeros, zeros, zeros))  60.8 us
    gather x96, local copies, waits for them, and re-layouts  59.5 us
    dynamic_update_slice x48, local copies, waits for them, and re-layouts, deposit(): lax.dynamic_update_slice(field, current + patch, (corner[0], corner[1]))  48.8 us
    unnamed x2, waiting for transfers between devices  28.8 us
    all_to_all x1, blocking collectives, local(): lax.all_to_all(fitted_here[:, :, None, :], 'ea', split_axis=1, concat_axi...  19.9 us
    add x46, other arithmetic, deposit(): current + patch  14.2 us
    all_to_all x1, starting transfers between devices, local(): lax.all_to_all(spectra, 'ea', split_axis=2, concat_axis=1, tiled=True)  13.8 us
    all_to_all x1, waiting for transfers between devices, local(): lax.all_to_all(spectra, 'ea', split_axis=2, concat_axis=1, tiled=True)  12 us
  transfers between devices with their start and end apart: 2, of which 2 were waited for; matrix products, arithmetic and copies ran while one was open for 2% of the time, Pallas kernels for 0%

commit v1 on v0

--- a/solution.py
+++ b/solution.py
@@ -1,3 +1,4 @@
+import functools
 import jax
 import jax.numpy as jnp
 from jax import lax
@@ -6,6 +7,18 @@
 HIGHEST_PRECISION = lax.Precision.HIGHEST
 FLOOR_POWER = 0.5
 REGULARIZER = 1.0
+
+
+def bench_push(here_x, which_axis):
+    return jnp.concatenate(
+        lax.all_to_all(
+            jnp.stack(jnp.split(here_x, lax.axis_size(which_axis), 1), 0), which_axis, 0, 0
+        ),
+        2,
+    )
+
+
+handle_case_for = functools.partial(bench_push, which_axis="ea")
 
 
 def dft_tables(length):
@@ -158,9 +171,7 @@
     fitted_here = jnp.einsum(
         "ke,ckn->cen", absorption_templates, coefs, precision=HIGHEST_PRECISION
     )
-    returned = lax.all_to_all(
-        fitted_here[:, :, None, :], "ea", split_axis=1, concat_axis=2, tiled=True
-    )
+    returned = handle_case_for(fitted_here[:, :, None, :])
     coef_local = coefs[:, :, None, :]
     return (returned[:, :, :, None, :], coef_local[:, :, 0, :])
 

time: 325 us -> 326 us (level)
  no operation moved by 1% of the time
where the time goes in v1:
time: 326 us; the launch traced here: 323 us
  local copies, waits for them, and re-layouts  123 us (38%)
  loops' own time  60.9 us (19%)
  waiting for transfers between devices  40.8 us (13%)
  matrix products  26.9 us (8%)
  other arithmetic  22.7 us (7%)
  blocking collectives  19.9 us (6%)
  between operations  15.3 us (5%)
  starting transfers between devices  13.8 us (4%)
    another operation x1, loops' own time, lone_wavelength(): return lax.fori_loop(0, rounds, advance, (zeros, zeros, zeros))  60.8 us
    gather x96, local copies, waits for them, and re-layouts  59.5 us
    dynamic_update_slice x48, local copies, waits for them, and re-layouts, deposit(): lax.dynamic_update_slice(field, current + patch, (corner[0], corner[1]))  48.8 us
    unnamed x2, waiting for transfers between devices  28.8 us
    all_to_all x1, blocking collectives, bench_push(): lax.all_to_all(jnp.stack(jnp.split(here_x, lax.axis_size(which_axis), 1),...  19.9 us
    add x46, other arithmetic, deposit(): current + patch  14.2 us
    all_to_all x1, starting transfers between devices, local(): lax.all_to_all(spectra, 'ea', split_axis=2, concat_axis=1, tiled=True)  13.8 us
    all_to_all x1, waiting for transfers between devices, local(): lax.all_to_all(spectra, 'ea', split_axis=2, concat_axis=1, tiled=True)  12 us
  transfers between devices with their start and end apart: 2, of which 2 were waited for; matrix products, arithmetic and copies ran while one was open for 2% of the time, Pallas kernels for 0%

profile of v1, /device:TPU:2, one launch (start us, length us, event | category | flops | bytes accessed | tf_op | source)
XLA Modules:
  0.0 323.3 jit_solution(16939474478106843490)
XLA Ops:
  10.6 216.4 %while.42 = (s32[]{:T(128)}, f32[256,256]{1,0:T(8,128)S(1)}, f32[256,256]{1,0:T(8,128)S(1)}, f32[256,256]{1,0:T(8,128)S(1)}, s32[]{:T(128)}, /*index=5*/s32[16,2...) while((s32[]{:T(128)}, f32[256,256]{1,0:T(8,128)S(1)}, ...), condition=%wide.region_5.6_spmd.clone.clone, body=%wide.region_1.5_spmd.clone.clone.sunk | while | flops 152179840 | bytes 5044471 | solution.py:134
  18.2 1.1 dynamic_update_slice.335
  29.1 1.1 dynamic_update_slice.337
  34.5 1.1 dynamic_update_slice.338
  57.4 14.9 %while.44 = (s32[]{:T(128)}, f32[256,256]{1,0:T(8,128)S(1)}, s32[8,2]{0,1:T(2,128)S(1)}, f32[8,32,32]{2,1,0:T(8,128)S(1)}, s32[]{:T(128)}) while((s32[]{:T(128)}, f32[256,256]{1,0:T(8,128)S(1)}, s32[8,2]{0,1:T(2,128)S(1)}, f32[8,32,32]{2,1,0:T(8,128)S(1)}, s32[]{:T(128)}) %tuple.143), condition=%wide.while_cond, body=%wide.while_body.sunk | while | flops 2 | bytes 32877 | solution.py:62
  58.0 1.3 bitcast_dynamic-update-slice_fusion.5
  59.9 1.3 bitcast_dynamic-update-slice_fusion.5
  61.7 1.3 bitcast_dynamic-update-slice_fusion.5
  63.6 1.3 bitcast_dynamic-update-slice_fusion.5
  65.5 1.3 bitcast_dynamic-update-slice_fusion.5
  67.3 1.3 bitcast_dynamic-update-slice_fusion.5
  69.2 1.3 bitcast_dynamic-update-slice_fusion.5
  71.0 1.3 bitcast_dynamic-update-slice_fusion.5
  72.3 14.9 %while.43 = (s32[]{:T(128)}, f32[256,256]{1,0:T(8,128)S(1)}, s32[8,2]{0,1:T(2,128)S(1)}, f32[8,32,32]{2,1,0:T(8,128)S(1)}, s32[]{:T(128)}) while((s32[]{:T(128)}, f32[256,256]{1,0:T(8,128)S(1)}, s32[8,2]{0,1:T(2,128)S(1)}, f32[8,32,32]{2,1,0:T(8,128)S(1)}, s32[]{:T(128)}) %tuple.153), condition=%wide.while_cond.1, body=%wide.while_body.1.sunk | while | flops 2 | bytes 32877 | solution.py:62
  72.9 1.3 bitcast_dynamic-update-slice_fusion.4
  74.8 1.3 bitcast_dynamic-update-slice_fusion.4
  76.7 1.3 bitcast_dynamic-update-slice_fusion.4
  78.5 1.3 bitcast_dynamic-update-slice_fusion.4
  80.4 1.3 bitcast_dynamic-update-slice_fusion.4
  82.2 1.3 bitcast_dynamic-update-slice_fusion.4
  84.1 1.3 bitcast_dynamic-update-slice_fusion.4
  86.0 1.3 bitcast_dynamic-update-slice_fusion.4
  100.9 1.1 dynamic_update_slice.327
  107.6 1.1 dynamic_update_slice.333
  109.6 1.1 dynamic_update_slice.319
  112.0 1.1 dynamic_update_slice.321
  113.2 1.1 dynamic_update_slice.322
  116.3 1.1 dynamic_update_slice.325
  131.3 1.1 dynamic_update_slice.336
  142.3 1.1 dynamic_update_slice.338
  147.8 1.1 dynamic_update_slice.339
  164.1 1.1 dynamic_update_slice.342
  165.4 14.9 %while.44 = (s32[]{:T(128)}, f32[256,256]{1,0:T(8,128)S(1)}, s32[8,2]{0,1:T(2,128)S(1)}, f32[8,32,32]{2,1,0:T(8,128)S(1)}, s32[]{:T(128)}) while((s32[]{:T(128)}, f32[256,256]{1,0:T(8,128)S(1)}, s32[8,2]{0,1:T(2,128)S(1)}, f32[8,32,32]{2,1,0:T(8,128)S(1)}, s32[]{:T(128)}) %tuple.143), condition=%wide.while_cond, body=%wide.while_body.sunk | while | flops 2 | bytes 32877 | solution.py:62
  166.0 1.3 bitcast_dynamic-update-slice_fusion.5
  167.9 1.3 bitcast_dynamic-update-slice_fusion.5
  169.7 1.3 bitcast_dynamic-update-slice_fusion.5
  171.6 1.3 bitcast_dynamic-update-slice_fusion.5
  173.5 1.3 bitcast_dynamic-update-slice_fusion.5
  175.3 1.3 bitcast_dynamic-update-slice_fusion.5
  177.2 1.3 bitcast_dynamic-update-slice_fusion.5
  179.0 1.3 bitcast_dynamic-update-slice_fusion.5
  180.3 14.9 %while.43 = (s32[]{:T(128)}, f32[256,256]{1,0:T(8,128)S(1)}, s32[8,2]{0,1:T(2,128)S(1)}, f32[8,32,32]{2,1,0:T(8,128)S(1)}, s32[]{:T(128)}) while((s32[]{:T(128)}, f32[256,256]{1,0:T(8,128)S(1)}, s32[8,2]{0,1:T(2,128)S(1)}, f32[8,32,32]{2,1,0:T(8,128)S(1)}, s32[]{:T(128)}) %tuple.153), condition=%wide.while_cond.1, body=%wide.while_body.1.sunk | while | flops 2 | bytes 32877 | solution.py:62
  180.9 1.3 bitcast_dynamic-update-slice_fusion.4
  182.8 1.3 bitcast_dynamic-update-slice_fusion.4
  184.7 1.3 bitcast_dynamic-update-slice_fusion.4
  186.5 1.3 bitcast_dynamic-update-slice_fusion.4
  188.4 1.3 bitcast_dynamic-update-slice_fusion.4
  190.2 1.3 bitcast_dynamic-update-slice_fusion.4
  192.1 1.3 bitcast_dynamic-update-slice_fusion.4
  194.0 1.3 bitcast_dynamic-update-slice_fusion.4
  208.9 1.1 dynamic_update_slice.327
  210.1 1.1 dynamic_update_slice.328
  211.3 1.1 dynamic_update_slice.329
  212.5 1.1 dynamic_update_slice.330
  213.7 1.1 dynamic_update_slice.331
  217.9 1.1 dynamic_update_slice.319
  219.1 1.1 dynamic_update_slice.320
  229.6 1.5 cholesky.16
  233.0 28.8 %all-reduce.3.cloned.1.call-done = f32[3,1,128,2,256]{4,2,3,1,0:T(8,128)} async-done(((f32[3,1,128,2,256]{4,2,3,1,0:T(8,128)}), f32[3,1,128,2,256]{4,2,3,1,0:T(8,128)}) %all-reduce.3.cloned.1.call-update) | async-done | bytes 786448
  261.8 1.7 constant_dynamic-slice_fusion.3
  264.9 13.8 %all-to-all-start = ((f32[2,1,128,256]{3,0,1,2:T(2,128)}), f32[2,1,128,256]{3,0,1,2:T(2,128)S(1)}, u32[]{:S(2)}, u32[]{:S(2)}) async-start(f32[2,1,128,256]{3,0,1,2:T(2,128)} %maximum_bitcast_fusion), calls=%async_computation | async-start | bytes 524288 | tf_op jit(solution)/shard_map/all_to_all | solution.py:169
  279.3 1.2 custom-call.10
  280.9 12.0 %all-to-all-done = f32[2,1,128,256]{3,0,1,2:T(2,128)S(1)} async-done(((f32[2,1,128,256]{3,0,1,2:T(2,128)}), f32[2,1,128,256]{3,0,1,2:T(2,128)S(1)}, u32[]{:S(2)}, u32[]{:S(2)}) %all-to-all-start) | async-done | bytes 262176 | tf_op jit(solution)/shard_map/all_to_all | solution.py:169
  295.6 19.9 %all_to_all.14 = f32[128,2,1,1,256]{4,2,3,1,0:T(1,128)S(1)} all-to-all(f32[128,2,1,1,256]{4,2,3,1,0:T(1,128)S(1)} %constant_dynamic-update-slice_fusion), channel_id=1, replica_groups=mesh['ea'=128,'ta'=2] {'ea'}, dimensions={0} | all-to-all | bytes 524288 | tf_op jit(solution)/shard_map/all_to_all | solution.py:14
  (372 shorter events, 106.2 us)
Async XLA Ops:
  7.2 222.2 %copy-start = (f32[16,128]{1,0:T(8,128)S(1)}, f32[16,128]{1,0:T(8,128)}, u32[]{:S(2)}) copy-start(f32[16,128]{1,0:T(8,128)} %param.17) | copy-start | bytes 24580
  7.2 254.6 %all-reduce.3.cloned.1.call-start = ((), (), s32[]{:S(2)}) async-start(), calls=%async_computation.2 | async-start | bytes 1572864
  7.9 0.7 copy-start.7
  8.7 1.0 copy-start.5
  9.5 1.0 copy-start.4
  9.6 1.0 copy-start.3
  9.6 1.0 copy-start.1
  9.6 1.0 copy-start.2
  231.1 0.7 copy-start.8
  264.9 28.0 %all-to-all-start = ((f32[2,1,128,256]{3,0,1,2:T(2,128)}), f32[2,1,128,256]{3,0,1,2:T(2,128)S(1)}, u32[]{:S(2)}, u32[]{:S(2)}) async-start(f32[2,1,128,256]{3,0,1,2:T(2,128)} %maximum_bitcast_fusion), calls=%async_computation | async-start | bytes 524288 | tf_op jit(solution)/shard_map/all_to_all | solution.py:169
  293.2 0.6 copy-start.6
Sparse Core Ops, SparseCore 0:
  229.0 32.7 all-reduce.2
